TPU v7x, 256 devices: a whole 4x4x8 slice. The times are simulated.
256 devices in a mesh: dp: 4 (over y), rows: 64 (over x, z, core).
Axes of the slice: x: 4, y: 4, z: 8, core: 2. Of those that a mesh axis runs over, the one named last changes fastest.
Arguments:
- grad: bfloat16 [4, 4096, 12288], P('dp', 'rows'), may hold values from -60 to 60
- error: bfloat16 [4, 4096, 12288], P('dp', 'rows'), may hold values from -3 to 3
- momentum: float32 [4096, 12288], P('rows'), may hold values from -3 to 3
- q_start: float32 [12288, 16], replicated, may hold values from -5 to 5
Outputs:
- new_error: bfloat16 [4, 4096, 12288], P('dp', 'rows')
- new_momentum: float32 [4096, 12288], P('rows')
- q_next: float32 [12288, 16], replicated
All inputs are finite; a program needn't handle non-finite values.
Results may differ from a plain program's by a relative error of at most 0.006.
Values sent between devices are 32-bit elements; how exact they have to be, the bound alone decides.
No kernel may reach another device: no remote copies, remote signals or barrier semaphores. Data moves between devices by JAX's collectives and lax.ppermute only.
A program may use at most 64 MiB of HBM per device.

v0:
```python
import functools
import jax
import jax.numpy as jnp
from jax import lax
from jax.experimental import pallas as pl
from jax.experimental.pallas import tpu as pltpu
from jax.sharding import Mesh, PartitionSpec as P

HIGHEST = lax.Precision.HIGHEST
F32 = jnp.float32
BF16 = jnp.bfloat16
LANES = 128
TILE = 8
WHOLE = pl.BlockSpec(memory_space=pltpu.VMEM)
FAR = pl.BlockSpec(memory_space=pltpu.HBM)


def split3(value):
    high = value.astype(BF16)
    rest = value - high.astype(F32)
    middle = rest.astype(BF16)
    low = (rest - middle.astype(F32)).astype(BF16)
    return high, middle, low


def nt_dot(first, second, precision=None):
    return lax.dot_general(
        first, second, (((1,), (1,)), ((), ())), precision=precision, preferred_element_type=F32
    )


def left_kernel(parts, grad, error, q_start, term, merged, base, grad_vmem, error_vmem, q_vmem, sems):
    unit = grad.shape[1] // sum(parts)
    slabs = [pl.ds(sum(parts[:step]) * unit, parts[step] * unit) for step in range(len(parts))]
    copies = []
    for step, here in enumerate(slabs):
        group = [
            pltpu.make_async_copy(far.at[:, here], near.at[:, here], sems.at[which, step])
            for which, (far, near) in enumerate(
                ((grad, grad_vmem), (error, error_vmem), (q_start, q_vmem))
            )
        ]
        for copy in group:
            copy.start()
        copies.append(group)
    total = jnp.zeros(term.shape, F32)
    for group, here in zip(copies, slabs):
        for copy in group:
            copy.wait()
        summed = grad_vmem[:, here].astype(F32) + error_vmem[:, here].astype(F32)
        base[:, here] = summed
        low = summed.astype(BF16)
        merged[:, here] = low
        total += nt_dot(q_vmem[:, here].astype(BF16), low)
    term[...] = total


def given_kernel(term, one, three, two, merged, given, gram, left):
    half = merged.shape[1] // 2
    rank = term.shape[0]
    total = (term[...] + two[...]) + (one[...] + three[...])
    left[...] = total
    there = pl.ds(pl.multiple_of((1 - lax.axis_index("core")) * half, LANES), half)
    given[:, :half] = jnp.dot(total.astype(BF16), merged[:, there], preferred_element_type=F32)
    square = nt_dot(total, total, HIGHEST)
    rest = jnp.zeros((TILE, LANES - 2 * rank), F32)
    tile = jnp.concatenate([square[:TILE], square[TILE:], rest], axis=1)
    gram[...] = tile
    given[:TILE, half:] = tile
    given[TILE:, half:] = jnp.zeros((rank - TILE, LANES), F32)


def kept_kernel(left, merged, kept):
    half = merged.shape[1] // 2
    here = pl.ds(pl.multiple_of(lax.axis_index("core") * half, LANES), half)
    kept[...] = jnp.dot(left[...].astype(BF16), merged[:, here], preferred_element_type=F32)


def pieces_kernel(kept, gram, taken, pieces):
    half = kept.shape[1]
    planes, tiles = pieces.shape[:2]
    across = (tiles - 1) // 2
    square = gram[...] + taken[:TILE, half:]
    for index in range(planes):
        for block in range(across):
            here = pl.ds((index * across + block) * LANES, LANES)
            total = kept[:, here] + taken[:, here]
            pieces[index, block] = total[:TILE]
            pieces[index, across + block] = total[TILE:]
        pieces[index, tiles - 1] = square


def plane_kernel(arrived, spread):
    total = arrived[0]
    for index in range(1, arrived.shape[0]):
        total += arrived[index]
    for index in range(spread.shape[0]):
        spread[index] = total


def layer_kernel(groups, arrived, spread, gram):
    tiles = spread.shape[1]
    total = arrived[0]
    for index in range(1, arrived.shape[0]):
        total += arrived[index]
    gram[...] = total[tiles] / groups
    for index in range(spread.shape[0]):
        spread[index] = total[:tiles]


def make_factors(groups, gram, left, factors):
    rank, rows = left.shape
    shape = (rank, LANES)
    row = lax.broadcasted_iota(jnp.int32, shape, 0)
    col = lax.broadcasted_iota(jnp.int32, shape, 1)
    third = (col >= rank) & (col < 2 * rank)
    square = jnp.concatenate([gram[:, :rank], gram[:, rank : 2 * rank]], axis=0)
    rest = jnp.zeros((rank, LANES - 2 * rank - rows), F32)
    table = jnp.concatenate([square, jnp.zeros((rank, rank), F32), left[...], rest], axis=1)
    table = jnp.where(col == row + rank, 1.0, table)
    pivots = jnp.ones(shape, F32)
    for step in range(rank):
        column = jnp.broadcast_to(table[:, step : step + 1], shape)
        scaled = table[step : step + 1, :] / column[step : step + 1, :]
        pivots = jnp.where(row == step, column, pivots)
        change = jnp.where((row < step) & third, 0.0, column * scaled)
        table = jnp.where(row == step, scaled, table - change)
    table = jnp.where(third, table * jnp.sqrt(pivots), table)
    combined = table[:, 2 * rank : 2 * rank + rows].T
    stacked = jnp.concatenate([combined, table[:, rank : 2 * rank]], axis=0) / groups
    high, middle, low = split3(stacked)
    factors[...] = jnp.concatenate([high, high, middle, high, middle, low], axis=1)


def put_halves(chunks, halves, factors, base, momentum, outs, scratch):
    error_vmem, momentum_vmem, q_vmem, sems = scratch
    rows, cols = base.shape
    half = cols // 2
    width = half // chunks
    copies = []
    for turn, (begin, source) in enumerate(halves):
        across = source.shape[1] // 2
        per = width // (across * LANES)
        for chunk in range(chunks):
            parts = []
            for index in range(chunk * per, (chunk + 1) * per):
                for block in range(across):
                    parts.append(jnp.concatenate([source[index, block], source[index, across + block]], axis=0))
            high, middle, low = split3(jnp.concatenate(parts, axis=1))
            depth = jnp.concatenate([high, middle, high, low, middle, high], axis=0)
            product = jnp.dot(factors[...], depth, preferred_element_type=F32)
            approx = product[:rows]
            here = pl.ds(turn * half + chunk * width, width)
            there = pl.ds(begin + chunk * width, width)
            q_vmem[:, here] = product[rows:]
            error_vmem[:, here] = (base[:, there] - approx).astype(BF16)
            momentum_vmem[:, here] = 0.9 * momentum[:, there] + approx
            for which, (near, far) in enumerate(zip((error_vmem, momentum_vmem, q_vmem), outs)):
                copy = pltpu.make_async_copy(
                    near.at[:, here], far.at[:, there], sems.at[which, turn * chunks + chunk]
                )
                copy.start()
                copies.append(copy)
    for copy in copies:
        copy.wait()


def ahead_kernel(groups, chunks, gram, left, own, base, momentum, factors, *rest):
    @pl.when(lax.axis_index("core") == 1)
    def _():
        make_factors(groups, gram, left, factors)
        half = base.shape[1] // 2
        put_halves(chunks, ((half, own),), factors, base, momentum, rest[:3], rest[3:])


def factor_kernel(groups, gram, left, factors):
    @pl.when(lax.axis_index("core") == 0)
    def _():
        make_factors(groups, gram, left, factors)


def output_kernel(chunks, ahead, beside, own, other, base, momentum, *rest):
    outs, scratch = rest[3:6], rest[6:]
    half = base.shape[1] // 2
    core = lax.axis_index("core")

    @pl.when(core == 0)
    def _():
        put_halves(chunks, ((0, own), (half, other)), beside, base, momentum, outs, scratch)

    @pl.when(core == 1)
    def _():
        put_halves(chunks, ((0, other),), ahead, base, momentum, outs, scratch)


def params(megabytes):
    return pltpu.CompilerParams(vmem_limit_bytes=megabytes * 1024 * 1024)


def cost(flops, moved):
    return pl.CostEstimate(flops=flops, bytes_accessed=moved, transcendentals=0)


def shards(grad, error, momentum, q_start):
    groups = lax.axis_size("dp")
    planes = groups * lax.axis_size("x")
    layers = lax.axis_size("z")
    cols, rank = q_start.shape
    rows = grad.shape[1]
    half = cols // 2
    tiles = rank * half // planes // (TILE * LANES)
    swap = [(0, 1), (1, 0)]
    parts = (1,) * 6

    term, merged, base = pl.pallas_call(
        functools.partial(left_kernel, parts),
        out_shape=(
            pltpu.VMEM((rank, rows), F32),
            pltpu.VMEM((rows, cols), BF16),
            pltpu.VMEM((rows, cols), F32),
        ),
        in_specs=[FAR] * 3,
        out_specs=(WHOLE,) * 3,
        scratch_shapes=[
            pltpu.VMEM((rows, cols), BF16),
            pltpu.VMEM((rows, cols), BF16),
            pltpu.VMEM((rank, cols), F32),
            pltpu.SemaphoreType.DMA((3, len(parts))),
        ],
        compiler_params=params(58),
        name="left_term",
    )(grad[0], error[0], q_start.T)
    one, three, two = (
        lax.ppermute(term, "dp", [(i, (i + k) % groups) for i in range(groups)]) for k in (1, 3, 2)
    )
    given, gram, left = pl.pallas_call(
        given_kernel,
        out_shape=(
            pltpu.VMEM((rank, half + LANES), F32),
            pltpu.VMEM((TILE, LANES), F32),
            pltpu.VMEM((rank, rows), F32),
        ),
        in_specs=[WHOLE] * 5,
        out_specs=(WHOLE,) * 3,
        compiler_params=params(8),
        name="right_given",
    )(term, one, three, two, merged)
    taken = lax.ppermute(given, "core", swap)
    kept = pl.pallas_call(
        kept_kernel,
        out_shape=pltpu.VMEM((rank, half), F32),
        in_specs=[WHOLE] * 2,
        out_specs=WHOLE,
        compiler_params=params(8),
        cost_estimate=cost(2 * rank * rows * half, 4 * rows * half),
        name="right_kept",
    )(left, merged)
    pieces = pl.pallas_call(
        pieces_kernel,
        out_shape=pltpu.VMEM((planes, tiles + 1, TILE, LANES), F32),
        in_specs=[WHOLE] * 3,
        out_specs=WHOLE,
        compiler_params=params(8),
        name="right_pieces",
    )(kept, gram, taken)
    arrived = lax.all_to_all(pieces, ("dp", "x"), 0, 0)
    spread = pl.pallas_call(
        plane_kernel,
        out_shape=pltpu.VMEM((layers, tiles + 1, TILE, LANES), F32),
        in_specs=[WHOLE],
        out_specs=WHOLE,
        compiler_params=params(8),
        name="plane_sum",
    )(arrived)
    arrived = lax.all_to_all(spread, "z", 0, 0)
    spread, gram = pl.pallas_call(
        functools.partial(layer_kernel, groups),
        out_shape=(pltpu.VMEM((planes, tiles, TILE, LANES), F32), pltpu.VMEM((TILE, LANES), F32)),
        in_specs=[WHOLE],
        out_specs=(WHOLE,) * 2,
        compiler_params=params(8),
        name="layer_sum",
    )(arrived)
    own = lax.all_to_all(spread, ("dp", "x"), 0, 0)
    chunks = 4
    shapes = (((rows, cols), BF16), ((rows, cols), F32), ((rank, cols), F32))
    out_shapes = tuple(jax.ShapeDtypeStruct(shape, dtype) for shape, dtype in shapes)
    factor_shape = pltpu.VMEM((rows + rank, 6 * rank), BF16)

    def scratch(halves):
        buffers = [pltpu.VMEM((shape[0], halves * half), dtype) for shape, dtype in shapes]
        return buffers + [pltpu.SemaphoreType.DMA((3, halves * chunks))]

    ahead, *begun = pl.pallas_call(
        functools.partial(ahead_kernel, groups, chunks),
        out_shape=(factor_shape,) + out_shapes,
        in_specs=[WHOLE] * 5,
        out_specs=(WHOLE,) + (FAR,) * 3,
        scratch_shapes=scratch(1),
        compiler_params=params(8),
        name="outputs_ahead",
    )(gram, left, own, base, momentum)
    own, ahead = lax.optimization_barrier((own, ahead))
    other = lax.ppermute(own, "core", swap)
    beside = pl.pallas_call(
        functools.partial(factor_kernel, groups),
        out_shape=factor_shape,
        in_specs=[WHOLE] * 2,
        out_specs=WHOLE,
        compiler_params=params(8),
        cost_estimate=cost(8 * rank * rows * LANES, 4 * rows * LANES),
        name="factors",
    )(gram, left)
    new_error, new_momentum, q_next = pl.pallas_call(
        functools.partial(output_kernel, chunks),
        out_shape=out_shapes,
        in_specs=[WHOLE] * 6 + [FAR] * 3,
        out_specs=(FAR,) * 3,
        scratch_shapes=scratch(2),
        input_output_aliases={6: 0, 7: 1, 8: 2},
        compiler_params=params(12),
        name="outputs",
    )(ahead, beside, own, other, base, momentum, *begun)
    return (new_error[None], new_momentum, q_next.T)


def solution(mesh):
    shape = mesh.shape
    fine = Mesh(mesh.devices.reshape(shape["dp"], 4, 8, 2), ("dp", "x", "z", "core"))
    rows = ("x", "z", "core")
    placed = (P("dp", rows, None), P("dp", rows, None), P(rows, None), P())
    return jax.shard_map(
        shards,
        mesh=fine,
        in_specs=placed,
        out_specs=(P("dp", rows, None), P(rows, None), P()),
        check_vma=False,
    )
```

profile of v0, /device:TPU:1, one launch (start us, length us, event | category | flops | bytes accessed | tf_op | source)
XLA Modules:
  0.0 66.4 jit_solution(5280881048903266227)
XLA Ops:
  0.6 2.5 %left_term.1 = (f32[16,64]{1,0:T(8,128)S(1)}, bf16[64,12288]{1,0:T(8,128)(2,1)S(1)}, f32[64,12288]{1,0:T(8,128)S(1)}) custom-call(bf16[64,12288]{1,0:T(8,128)(2,1)} %bitcast.5, bf16[64,12288]{1,0:T(8,128)(2,1)} %bitcast.6, f32[16,12288]{1,0:T(8,128)} %bitcast.8), custom_call_target="tpu_custom_call" | custom-call | tf_op jit(solution)/shard_map/left_term/pallas_call | solution.py:215
  3.2 3.8 %collective-permute-start.2 = (f32[16,64]{1,0:T(8,128)S(1)}, f32[16,64]{1,0:T(8,128)S(1)}, u32[]{:S(2)}, u32[]{:S(2)}) collective-permute-start(f32[16,64]{1,0:T(8,128)S(1)} %get-tuple-element.20.term), channel_id=1, source_target_pairs={{0,128},{64,192},{128,0},{192,64},{1,129},{65,193},{129,1},{193,65... | collective-permute-start | bytes 12296 | tf_op jit(solution)/shard_map/ppermute | solution.py:234
  7.0 0.8 %collective-permute-start.1 = (f32[16,64]{1,0:T(8,128)S(1)}, f32[16,64]{1,0:T(8,128)S(1)}, u32[]{:S(2)}, u32[]{:S(2)}) collective-permute-start(f32[16,64]{1,0:T(8,128)S(1)} %get-tuple-element.20.term), channel_id=1, source_target_pairs={{0,192},{64,0},{128,64},{192,128},{1,193},{65,1},{129,65},{193,129... | collective-permute-start | bytes 12296 | tf_op jit(solution)/shard_map/ppermute | solution.py:234
  7.8 0.7 %collective-permute-start = (f32[16,64]{1,0:T(8,128)S(1)}, f32[16,64]{1,0:T(8,128)S(1)}, u32[]{:S(2)}, u32[]{:S(2)}) collective-permute-start(f32[16,64]{1,0:T(8,128)S(1)} %get-tuple-element.20.term), channel_id=1, source_target_pairs={{0,64},{64,128},{128,192},{192,0},{1,65},{65,129},{129,193},{193,1... | collective-permute-start | bytes 12296 | tf_op jit(solution)/shard_map/ppermute | solution.py:234
  8.5 0.0 collective-permute-done.2.two
  8.5 1.0 %collective-permute-done.1.three = f32[16,64]{1,0:T(8,128)S(1)} collective-permute-done((f32[16,64]{1,0:T(8,128)S(1)}, f32[16,64]{1,0:T(8,128)S(1)}, u32[]{:S(2)}, u32[]{:S(2)}) %collective-permute-start.1) | collective-permute-done | bytes 4128 | tf_op jit(solution)/shard_map/ppermute | solution.py:234
  9.5 2.0 %collective-permute-done.one = f32[16,64]{1,0:T(8,128)S(1)} collective-permute-done((f32[16,64]{1,0:T(8,128)S(1)}, f32[16,64]{1,0:T(8,128)S(1)}, u32[]{:S(2)}, u32[]{:S(2)}) %collective-permute-start) | collective-permute-done | bytes 4128 | tf_op jit(solution)/shard_map/ppermute | solution.py:234
  11.5 0.3 right_given.1
  11.8 2.4 %collective-permute-start.3 = (f32[16,6272]{1,0:T(8,128)S(1)}, f32[16,6272]{1,0:T(8,128)S(1)}, u32[]{:S(2)}, u32[]{:S(2)}) collective-permute-start(f32[16,6272]{1,0:T(8,128)S(1)} %get-tuple-element.24), channel_id=1, source_target_pairs={{0,1},{1,0},{2,3},{3,2},{4,5},{5,4},{6,7},{7,6},{8,9},{9,8},{10,11... | collective-permute-start | bytes 1204232 | tf_op jit(solution)/shard_map/ppermute | solution.py:248
  14.2 0.2 right_kept.1.kept
  14.4 1.1 %collective-permute-done.3.taken = f32[16,6272]{1,0:T(8,128)S(1)} collective-permute-done((f32[16,6272]{1,0:T(8,128)S(1)}, f32[16,6272]{1,0:T(8,128)S(1)}, u32[]{:S(2)}, u32[]{:S(2)}) %collective-permute-start.3) | collective-permute-done | bytes 401440 | tf_op jit(solution)/shard_map/ppermute | solution.py:248
  15.6 0.0 copy-start
  15.6 0.1 right_pieces.1
  15.6 14.1 %all_to_all.15.arrived = f32[16,7,8,128]{3,2,1,0:T(8,128)S(1)} all-to-all(f32[16,7,8,128]{3,2,1,0:T(8,128)S(1)} %right_pieces.1), channel_id=1, replica_groups=mesh['dp'=4,'x'=4,'z'=8,'core'=2] {'dp','x'}, dimensions={0} | all-to-all | bytes 917504 | tf_op jit(solution)/shard_map/all_to_all | solution.py:266
  29.8 17.1 %all_to_all.16.arrived = f32[8,7,8,128]{3,2,1,0:T(8,128)S(1)} all-to-all(f32[8,7,8,128]{3,2,1,0:T(8,128)S(1)} %plane_sum.1), channel_id=1, replica_groups=mesh['dp'=4,'x'=4,'z'=8,'core'=2] {'z'}, dimensions={0} | all-to-all | bytes 458752 | tf_op jit(solution)/shard_map/all_to_all | solution.py:275
  46.9 11.9 %all_to_all.17.own = f32[16,6,8,128]{3,2,1,0:T(8,128)S(1)} all-to-all(f32[16,6,8,128]{3,2,1,0:T(8,128)S(1)} %get-tuple-element.25), channel_id=1, replica_groups=mesh['dp'=4,'x'=4,'z'=8,'core'=2] {'dp','x'}, dimensions={0} | all-to-all | bytes 786432 | tf_op jit(solution)/shard_map/all_to_all | solution.py:284
  58.8 0.0 copy-done
  58.8 3.5 %outputs_ahead.1 = (bf16[80,96]{1,0:T(8,128)(2,1)S(1)}, bf16[64,12288]{1,0:T(8,128)(2,1)}, f32[64,12288]{1,0:T(8,128)}, f32[16,12288]{1,0:T(8,128)}) custom-call(f32[8,128]{1,0:T(8,128)S(1)} %get-tuple-element.26.gram, f32[16,64]{1,0:T(8,128)S(1)} %get-tuple-element.22.left, f32[16,6,8,128]{3,2,1,0:T(8,128)S(1)} %all_to_all.17.own, ...), custom_call_target="tpu_custom_call" | custom-call | tf_op jit(solution)/shard_map/outputs_ahead/pallas_call | solution.py:294
  62.2 0.9 %collective-permute-start.4 = (f32[16,6,8,128]{3,2,1,0:T(8,128)S(1)}, f32[16,6,8,128]{3,2,1,0:T(8,128)S(1)}, u32[]{:S(2)}, u32[]{:S(2)}) collective-permute-start(f32[16,6,8,128]{3,2,1,0:T(8,128)S(1)} %all_to_all.17.own), channel_id=1, source_target_pairs={{0,1},{1,0},{2,3},{3,2},{4,5},{5,4},{6,7},{7,6},{8,9},{9,8},{10,11... | collective-permute-start | bytes 1179656 | tf_op jit(solution)/shard_map/ppermute | solution.py:304
  63.1 1.3 %collective-permute-done.4.other = f32[16,6,8,128]{3,2,1,0:T(8,128)S(1)} collective-permute-done((f32[16,6,8,128]{3,2,1,0:T(8,128)S(1)}, f32[16,6,8,128]{3,2,1,0:T(8,128)S(1)}, u32[]{:S(2)}, u32[]{:S(2)}) %collective-permute-start.4) | collective-permute-done | bytes 393248 | tf_op jit(solution)/shard_map/ppermute | solution.py:304
  64.4 2.0 %outputs.1 = (bf16[64,12288]{1,0:T(8,128)(2,1)}, f32[64,12288]{1,0:T(8,128)}, f32[16,12288]{1,0:T(8,128)}) custom-call(bf16[80,96]{1,0:T(8,128)(2,1)S(1)} %get-tuple-element.29.ahead, bf16[80,96]{1,0:T(8,128)(2,1)S(1)} %factors.1.beside, f32[16,6,8,128]{3,2,1,0:T(8,128)S(1)} %all_to_all.17.own, ...), custom_call_target="tpu_custom_call", output_to_operand_aliasing={{0}: (6, {}), {1}: (7, {}), {2}: (8, {})} | custom-call | tf_op jit(solution)/shard_map/outputs/pallas_call | solution.py:314
  (3 shorter events, 0.1 us)
Async XLA Ops:
  3.2 5.3 %collective-permute-start.2 = (f32[16,64]{1,0:T(8,128)S(1)}, f32[16,64]{1,0:T(8,128)S(1)}, u32[]{:S(2)}, u32[]{:S(2)}) collective-permute-start(f32[16,64]{1,0:T(8,128)S(1)} %get-tuple-element.20.term), channel_id=1, source_target_pairs={{0,128},{64,192},{128,0},{192,64},{1,129},{65,193},{129,1},{193,65... | collective-permute-start | bytes 12296 | tf_op jit(solution)/shard_map/ppermute | solution.py:234
  7.0 2.5 %collective-permute-start.1 = (f32[16,64]{1,0:T(8,128)S(1)}, f32[16,64]{1,0:T(8,128)S(1)}, u32[]{:S(2)}, u32[]{:S(2)}) collective-permute-start(f32[16,64]{1,0:T(8,128)S(1)} %get-tuple-element.20.term), channel_id=1, source_target_pairs={{0,192},{64,0},{128,64},{192,128},{1,193},{65,1},{129,65},{193,129... | collective-permute-start | bytes 12296 | tf_op jit(solution)/shard_map/ppermute | solution.py:234
  7.8 3.7 %collective-permute-start = (f32[16,64]{1,0:T(8,128)S(1)}, f32[16,64]{1,0:T(8,128)S(1)}, u32[]{:S(2)}, u32[]{:S(2)}) collective-permute-start(f32[16,64]{1,0:T(8,128)S(1)} %get-tuple-element.20.term), channel_id=1, source_target_pairs={{0,64},{64,128},{128,192},{192,0},{1,65},{65,129},{129,193},{193,1... | collective-permute-start | bytes 12296 | tf_op jit(solution)/shard_map/ppermute | solution.py:234
  11.8 3.8 %collective-permute-start.3 = (f32[16,6272]{1,0:T(8,128)S(1)}, f32[16,6272]{1,0:T(8,128)S(1)}, u32[]{:S(2)}, u32[]{:S(2)}) collective-permute-start(f32[16,6272]{1,0:T(8,128)S(1)} %get-tuple-element.24), channel_id=1, source_target_pairs={{0,1},{1,0},{2,3},{3,2},{4,5},{5,4},{6,7},{7,6},{8,9},{9,8},{10,11... | collective-permute-start | bytes 1204232 | tf_op jit(solution)/shard_map/ppermute | solution.py:248
  15.6 43.2 %copy-start = (f32[64,12288]{1,0:T(8,128)S(1)}, f32[64,12288]{1,0:T(8,128)}, u32[]{:S(2)}) copy-start(f32[64,12288]{1,0:T(8,128)} %momentum.3) | copy-start | bytes 9437188
  62.2 2.2 %collective-permute-start.4 = (f32[16,6,8,128]{3,2,1,0:T(8,128)S(1)}, f32[16,6,8,128]{3,2,1,0:T(8,128)S(1)}, u32[]{:S(2)}, u32[]{:S(2)}) collective-permute-start(f32[16,6,8,128]{3,2,1,0:T(8,128)S(1)} %all_to_all.17.own), channel_id=1, source_target_pairs={{0,1},{1,0},{2,3},{3,2},{4,5},{5,4},{6,7},{7,6},{8,9},{9,8},{10,11... | collective-permute-start | bytes 1179656 | tf_op jit(solution)/shard_map/ppermute | solution.py:304
where the time goes:
time: 66.6 us; the launch traced here: 66.4 us
  blocking collectives  43.1 us (65%)
  Pallas kernels  8.58 us (13%)
  starting transfers between devices  8.57 us (13%)
  waiting for transfers between devices  5.51 us (8%)
    all_to_all x1, blocking collectives, shards(): arrived = lax.all_to_all(spread, 'z', 0, 0)  17.1 us
    all_to_all x1, blocking collectives, shards(): arrived = lax.all_to_all(pieces, ('dp', 'x'), 0, 0)  14.1 us
    all_to_all x1, blocking collectives, shards(): own = lax.all_to_all(spread, ('dp', 'x'), 0, 0)  11.9 us
    ppermute x3, starting transfers between devices, shards(): lax.ppermute(term, 'dp', [(i, (i + k) % groups) for i in range(groups)])  5.3 us
    pallas_call x1, Pallas kernels, shards(): pl.pallas_call(functools.partial(ahead_kernel, groups, chunks), out_shape...  3.45 us
    ppermute x3, waiting for transfers between devices, shards(): lax.ppermute(term, 'dp', [(i, (i + k) % groups) for i in range(groups)])  3.02 us
    pallas_call x1, Pallas kernels, shards(): pl.pallas_call(functools.partial(left_kernel, parts), out_shape=(pltpu.VM...  2.53 us
    ppermute x1, starting transfers between devices, shards(): taken = lax.ppermute(given, 'core', swap)  2.41 us
  transfers between devices with their start and end apart: 5, of which 4 were waited for; matrix products, arithmetic and copies ran while one was open for 0% of the time, Pallas kernels for 0%

commit v1 on v0

--- a/solution.py
+++ b/solution.py
@@ -201,6 +201,11 @@
     return pl.CostEstimate(flops=flops, bytes_accessed=moved, transcendentals=0)
 
 
+def exchange(array, axes):
+    flat = array.reshape(array.shape[0], -1, LANES)
+    return lax.all_to_all(flat, axes, 0, 0).reshape(array.shape)
+
+
 def shards(grad, error, momentum, q_start):
     groups = lax.axis_size("dp")
     planes = groups * lax.axis_size("x")
@@ -263,7 +268,7 @@
         compiler_params=params(8),
         name="right_pieces",
     )(kept, gram, taken)
-    arrived = lax.all_to_all(pieces, ("dp", "x"), 0, 0)
+    arrived = exchange(pieces, ("dp", "x"))
     spread = pl.pallas_call(
         plane_kernel,
         out_shape=pltpu.VMEM((layers, tiles + 1, TILE, LANES), F32),
@@ -272,7 +277,7 @@
         compiler_params=params(8),
         name="plane_sum",
     )(arrived)
-    arrived = lax.all_to_all(spread, "z", 0, 0)
+    arrived = exchange(spread, "z")
     spread, gram = pl.pallas_call(
         functools.partial(layer_kernel, groups),
         out_shape=(pltpu.VMEM((planes, tiles, TILE, LANES), F32), pltpu.VMEM((TILE, LANES), F32)),
@@ -281,7 +286,7 @@
         compiler_params=params(8),
         name="layer_sum",
     )(arrived)
-    own = lax.all_to_all(spread, ("dp", "x"), 0, 0)
+    own = exchange(spread, ("dp", "x"))
     chunks = 4
     shapes = (((rows, cols), BF16), ((rows, cols), F32), ((rank, cols), F32))
     out_shapes = tuple(jax.ShapeDtypeStruct(shape, dtype) for shape, dtype in shapes)

time: 66.6 us -> 66.6 us (level)
  no operation moved by 1% of the time
where the time goes in v1:
time: 66.6 us; the launch traced here: 66.4 us
  blocking collectives  43.1 us (65%)
  Pallas kernels  8.58 us (13%)
  starting transfers between devices  8.57 us (13%)
  waiting for transfers between devices  5.51 us (8%)
    all_to_all x3, blocking collectives, exchange(): return lax.all_to_all(flat, axes, 0, 0).reshape(array.shape)  43.1 us
    ppermute x3, starting transfers between devices, shards(): lax.ppermute(term, 'dp', [(i, (i + k) % groups) for i in range(groups)])  5.3 us
    pallas_call x1, Pallas kernels, shards(): pl.pallas_call(functools.partial(ahead_kernel, groups, chunks), out_shape...  3.45 us
    ppermute x3, waiting for transfers between devices, shards(): lax.ppermute(term, 'dp', [(i, (i + k) % groups) for i in range(groups)])  3.02 us
    pallas_call x1, Pallas kernels, shards(): pl.pallas_call(functools.partial(left_kernel, parts), out_shape=(pltpu.VM...  2.53 us
    ppermute x1, starting transfers between devices, shards(): taken = lax.ppermute(given, 'core', swap)  2.41 us
    pallas_call x1, Pallas kernels, shards(): pl.pallas_call(functools.partial(output_kernel, chunks), out_shape=out_sh...  1.95 us
    ppermute x1, waiting for transfers between devices, shards(): other = lax.ppermute(own, 'core', swap)  1.35 us
  transfers between devices with their start and end apart: 5, of which 4 were waited for; matrix products, arithmetic and copies ran while one was open for 0% of the time, Pallas kernels for 0%

profile of v1, /device:TPU:1, one launch (start us, length us, event | category | flops | bytes accessed | tf_op | source)
XLA Modules:
  0.0 66.4 jit_solution(6798890470502628263)
XLA Ops:
  0.6 2.5 %left_term.1 = (f32[16,64]{1,0:T(8,128)S(1)}, bf16[64,12288]{1,0:T(8,128)(2,1)S(1)}, f32[64,12288]{1,0:T(8,128)S(1)}) custom-call(bf16[64,12288]{1,0:T(8,128)(2,1)} %bitcast.19, bf16[64,12288]{1,0:T(8,128)(2,1)} %bitcast.20, f32[16,12288]{1,0:T(8,128)} %bitcast.22), custom_call_target="tpu_custom_call" | custom-call | tf_op jit(solution)/shard_map/left_term/pallas_call | solution.py:220
  3.2 3.8 %collective-permute-start.2 = (f32[16,64]{1,0:T(8,128)S(1)}, f32[16,64]{1,0:T(8,128)S(1)}, u32[]{:S(2)}, u32[]{:S(2)}) collective-permute-start(f32[16,64]{1,0:T(8,128)S(1)} %get-tuple-element.20.term), channel_id=1, source_target_pairs={{0,128},{64,192},{128,0},{192,64},{1,129},{65,193},{129,1},{193,65... | collective-permute-start | bytes 12296 | tf_op jit(solution)/shard_map/ppermute | solution.py:239
  7.0 0.8 %collective-permute-start.1 = (f32[16,64]{1,0:T(8,128)S(1)}, f32[16,64]{1,0:T(8,128)S(1)}, u32[]{:S(2)}, u32[]{:S(2)}) collective-permute-start(f32[16,64]{1,0:T(8,128)S(1)} %get-tuple-element.20.term), channel_id=1, source_target_pairs={{0,192},{64,0},{128,64},{192,128},{1,193},{65,1},{129,65},{193,129... | collective-permute-start | bytes 12296 | tf_op jit(solution)/shard_map/ppermute | solution.py:239
  7.8 0.7 %collective-permute-start = (f32[16,64]{1,0:T(8,128)S(1)}, f32[16,64]{1,0:T(8,128)S(1)}, u32[]{:S(2)}, u32[]{:S(2)}) collective-permute-start(f32[16,64]{1,0:T(8,128)S(1)} %get-tuple-element.20.term), channel_id=1, source_target_pairs={{0,64},{64,128},{128,192},{192,0},{1,65},{65,129},{129,193},{193,1... | collective-permute-start | bytes 12296 | tf_op jit(solution)/shard_map/ppermute | solution.py:239
  8.5 0.0 collective-permute-done.2.two
  8.5 1.0 %collective-permute-done.1.three = f32[16,64]{1,0:T(8,128)S(1)} collective-permute-done((f32[16,64]{1,0:T(8,128)S(1)}, f32[16,64]{1,0:T(8,128)S(1)}, u32[]{:S(2)}, u32[]{:S(2)}) %collective-permute-start.1) | collective-permute-done | bytes 4128 | tf_op jit(solution)/shard_map/ppermute | solution.py:239
  9.5 2.0 %collective-permute-done.one = f32[16,64]{1,0:T(8,128)S(1)} collective-permute-done((f32[16,64]{1,0:T(8,128)S(1)}, f32[16,64]{1,0:T(8,128)S(1)}, u32[]{:S(2)}, u32[]{:S(2)}) %collective-permute-start) | collective-permute-done | bytes 4128 | tf_op jit(solution)/shard_map/ppermute | solution.py:239
  11.5 0.3 right_given.1
  11.8 2.4 %collective-permute-start.3 = (f32[16,6272]{1,0:T(8,128)S(1)}, f32[16,6272]{1,0:T(8,128)S(1)}, u32[]{:S(2)}, u32[]{:S(2)}) collective-permute-start(f32[16,6272]{1,0:T(8,128)S(1)} %get-tuple-element.24), channel_id=1, source_target_pairs={{0,1},{1,0},{2,3},{3,2},{4,5},{5,4},{6,7},{7,6},{8,9},{9,8},{10,11... | collective-permute-start | bytes 1204232 | tf_op jit(solution)/shard_map/ppermute | solution.py:253
  14.2 0.2 right_kept.1.kept
  14.4 1.1 %collective-permute-done.3.taken = f32[16,6272]{1,0:T(8,128)S(1)} collective-permute-done((f32[16,6272]{1,0:T(8,128)S(1)}, f32[16,6272]{1,0:T(8,128)S(1)}, u32[]{:S(2)}, u32[]{:S(2)}) %collective-permute-start.3) | collective-permute-done | bytes 401440 | tf_op jit(solution)/shard_map/ppermute | solution.py:253
  15.6 0.0 copy-start
  15.6 0.1 right_pieces.1
  15.6 14.1 %all_to_all.15 = f32[16,56,128]{2,1,0:T(8,128)S(1)} all-to-all(f32[16,56,128]{2,1,0:T(8,128)S(1)} %bitcast.14), channel_id=1, replica_groups=mesh['dp'=4,'x'=4,'z'=8,'core'=2] {'dp','x'}, dimensions={0} | all-to-all | bytes 917504 | tf_op jit(solution)/shard_map/all_to_all | solution.py:206
  29.8 17.1 %all_to_all.16 = f32[8,56,128]{2,1,0:T(8,128)S(1)} all-to-all(f32[8,56,128]{2,1,0:T(8,128)S(1)} %bitcast.17), channel_id=1, replica_groups=mesh['dp'=4,'x'=4,'z'=8,'core'=2] {'z'}, dimensions={0} | all-to-all | bytes 458752 | tf_op jit(solution)/shard_map/all_to_all | solution.py:206
  46.9 11.9 %all_to_all.17 = f32[16,48,128]{2,1,0:T(8,128)S(1)} all-to-all(f32[16,48,128]{2,1,0:T(8,128)S(1)} %bitcast.18), channel_id=1, replica_groups=mesh['dp'=4,'x'=4,'z'=8,'core'=2] {'dp','x'}, dimensions={0} | all-to-all | bytes 786432 | tf_op jit(solution)/shard_map/all_to_all | solution.py:206
  58.8 0.0 copy-done
  58.8 3.5 %outputs_ahead.1 = (bf16[80,96]{1,0:T(8,128)(2,1)S(1)}, bf16[64,12288]{1,0:T(8,128)(2,1)}, f32[64,12288]{1,0:T(8,128)}, f32[16,12288]{1,0:T(8,128)}) custom-call(f32[8,128]{1,0:T(8,128)S(1)} %get-tuple-element.26.gram, f32[16,64]{1,0:T(8,128)S(1)} %get-tuple-element.22.left, f32[16,6,8,128]{3,2,1,0:T(8,128)S(1)} %bitcast.11, ...), custom_call_target="tpu_custom_call" | custom-call | tf_op jit(solution)/shard_map/outputs_ahead/pallas_call | solution.py:299
  62.2 0.9 %collective-permute-start.4 = (f32[16,6,8,128]{3,2,1,0:T(8,128)S(1)}, f32[16,6,8,128]{3,2,1,0:T(8,128)S(1)}, u32[]{:S(2)}, u32[]{:S(2)}) collective-permute-start(f32[16,6,8,128]{3,2,1,0:T(8,128)S(1)} %bitcast.12), channel_id=1, source_target_pairs={{0,1},{1,0},{2,3},{3,2},{4,5},{5,4},{6,7},{7,6},{8,9},{9,8},{10,11... | collective-permute-start | bytes 1179656 | tf_op jit(solution)/shard_map/ppermute | solution.py:309
  63.1 1.3 %collective-permute-done.4.other = f32[16,6,8,128]{3,2,1,0:T(8,128)S(1)} collective-permute-done((f32[16,6,8,128]{3,2,1,0:T(8,128)S(1)}, f32[16,6,8,128]{3,2,1,0:T(8,128)S(1)}, u32[]{:S(2)}, u32[]{:S(2)}) %collective-permute-start.4) | collective-permute-done | bytes 393248 | tf_op jit(solution)/shard_map/ppermute | solution.py:309
  64.4 2.0 %outputs.1 = (bf16[64,12288]{1,0:T(8,128)(2,1)}, f32[64,12288]{1,0:T(8,128)}, f32[16,12288]{1,0:T(8,128)}) custom-call(bf16[80,96]{1,0:T(8,128)(2,1)S(1)} %get-tuple-element.29.ahead, bf16[80,96]{1,0:T(8,128)(2,1)S(1)} %factors.1.beside, f32[16,6,8,128]{3,2,1,0:T(8,128)S(1)} %bitcast.13, ...), custom_call_target="tpu_custom_call", output_to_operand_aliasing={{0}: (6, {}), {1}: (7, {}), {2}: (8, {})} | custom-call | tf_op jit(solution)/shard_map/outputs/pallas_call | solution.py:319
  (3 shorter events, 0.1 us)
Async XLA Ops:
  3.2 5.3 %collective-permute-start.2 = (f32[16,64]{1,0:T(8,128)S(1)}, f32[16,64]{1,0:T(8,128)S(1)}, u32[]{:S(2)}, u32[]{:S(2)}) collective-permute-start(f32[16,64]{1,0:T(8,128)S(1)} %get-tuple-element.20.term), channel_id=1, source_target_pairs={{0,128},{64,192},{128,0},{192,64},{1,129},{65,193},{129,1},{193,65... | collective-permute-start | bytes 12296 | tf_op jit(solution)/shard_map/ppermute | solution.py:239
  7.0 2.5 %collective-permute-start.1 = (f32[16,64]{1,0:T(8,128)S(1)}, f32[16,64]{1,0:T(8,128)S(1)}, u32[]{:S(2)}, u32[]{:S(2)}) collective-permute-start(f32[16,64]{1,0:T(8,128)S(1)} %get-tuple-element.20.term), channel_id=1, source_target_pairs={{0,192},{64,0},{128,64},{192,128},{1,193},{65,1},{129,65},{193,129... | collective-permute-start | bytes 12296 | tf_op jit(solution)/shard_map/ppermute | solution.py:239
  7.8 3.7 %collective-permute-start = (f32[16,64]{1,0:T(8,128)S(1)}, f32[16,64]{1,0:T(8,128)S(1)}, u32[]{:S(2)}, u32[]{:S(2)}) collective-permute-start(f32[16,64]{1,0:T(8,128)S(1)} %get-tuple-element.20.term), channel_id=1, source_target_pairs={{0,64},{64,128},{128,192},{192,0},{1,65},{65,129},{129,193},{193,1... | collective-permute-start | bytes 12296 | tf_op jit(solution)/shard_map/ppermute | solution.py:239
  11.8 3.8 %collective-permute-start.3 = (f32[16,6272]{1,0:T(8,128)S(1)}, f32[16,6272]{1,0:T(8,128)S(1)}, u32[]{:S(2)}, u32[]{:S(2)}) collective-permute-start(f32[16,6272]{1,0:T(8,128)S(1)} %get-tuple-element.24), channel_id=1, source_target_pairs={{0,1},{1,0},{2,3},{3,2},{4,5},{5,4},{6,7},{7,6},{8,9},{9,8},{10,11... | collective-permute-start | bytes 1204232 | tf_op jit(solution)/shard_map/ppermute | solution.py:253
  15.6 43.2 %copy-start = (f32[64,12288]{1,0:T(8,128)S(1)}, f32[64,12288]{1,0:T(8,128)}, u32[]{:S(2)}) copy-start(f32[64,12288]{1,0:T(8,128)} %momentum.3) | copy-start | bytes 9437188
  62.2 2.2 %collective-permute-start.4 = (f32[16,6,8,128]{3,2,1,0:T(8,128)S(1)}, f32[16,6,8,128]{3,2,1,0:T(8,128)S(1)}, u32[]{:S(2)}, u32[]{:S(2)}) collective-permute-start(f32[16,6,8,128]{3,2,1,0:T(8,128)S(1)} %bitcast.12), channel_id=1, source_target_pairs={{0,1},{1,0},{2,3},{3,2},{4,5},{5,4},{6,7},{7,6},{8,9},{9,8},{10,11... | collective-permute-start | bytes 1179656 | tf_op jit(solution)/shard_map/ppermute | solution.py:309
